TPU v7x, 512 devices: a whole 4x4x16 slice. The times are simulated.
512 devices in a mesh: tm: 16 (over x_lo, y, core), patch: 32 (over z, x_hi).
Axes of the slice: x: 4 (x_hi: 2, x_lo: 2; x = x_hi * 2 + x_lo), y: 4, z: 16, core: 2. Of those that a mesh axis runs over, the one named last changes fastest.
Arguments:
- query_vectors: bfloat16 [16, 16, 256, 2048], P(None, 'tm', 'patch'), may hold values from -32 to 32
- key_vectors: bfloat16 [16, 16, 256, 2048], P(None, 'tm', 'patch'), may hold values from -32 to 32
- value_vectors: bfloat16 [16, 16, 256, 2048], P(None, 'tm', 'patch'), may hold values from -6 to 6
- grad_output: bfloat16 [16, 16, 256, 2048], P(None, 'tm', 'patch'), may hold values from -6 to 6
- time_bias: float32 [16, 16], replicated, may hold values from -26 to 2
Outputs:
- grad_queries: bfloat16 [16, 16, 256, 2048], P(None, 'tm', 'patch')
- grad_keys: bfloat16 [16, 16, 256, 2048], P(None, 'tm', 'patch')
- grad_values: bfloat16 [16, 16, 256, 2048], P(None, 'tm', 'patch')
- grad_bias: float32 [16, 16], replicated
All inputs are finite; a program needn't handle non-finite values.
Results may differ from a plain program's by a relative error of at most 0.0069.
Values may be sent and summed in bfloat16 or wider, within the bound.
A program may use at most 64 MiB of HBM per device.

v0:
```python
import math

import jax
import jax.numpy as jnp
from jax import lax
from jax.sharding import PartitionSpec as P


def score_table(bias_rows, frames):
    steps = jnp.arange(frames, dtype=jnp.int32)
    offsets = steps[:, None] - steps[None, :]
    onehot = (offsets[:, :, None] == steps[None, None, :]).astype(jnp.float32)
    table = jnp.einsum("hd,tud->htu", bias_rows, onehot, precision=lax.Precision.HIGHEST)
    return (table, offsets >= 0, onehot)


def attend_back(query_heads, key_heads, value_heads, grad_heads, bias_rows):
    frames = query_heads.shape[1]
    score_scale = 1.0 / math.sqrt(query_heads.shape[4])
    table, causal, onehot = score_table(bias_rows, frames)
    scores = (
        jnp.einsum("atxhd,auxhd->axhtu", query_heads, key_heads, preferred_element_type=jnp.float32)
        * score_scale
        + table[None, None]
    )
    scores = jnp.where(causal, scores, -jnp.inf)
    row_max = jnp.max(scores, axis=-1, keepdims=True)
    expon = jnp.exp(scores - row_max)
    weights = expon / jnp.sum(expon, axis=-1, keepdims=True)
    weights_low = weights.astype(jnp.bfloat16)
    attended = jnp.einsum(
        "axhtu,auxhd->atxhd", weights_low, value_heads, preferred_element_type=jnp.float32
    )
    rowdot = jnp.einsum(
        "atxhd,atxhd->axht", grad_heads, attended, preferred_element_type=jnp.float32
    )
    grad_weights = jnp.einsum(
        "atxhd,auxhd->axhtu", grad_heads, value_heads, preferred_element_type=jnp.float32
    )
    grad_scores = weights * (grad_weights - rowdot[..., None])
    bias_terms = jnp.einsum("axhtu,tud->axhd", grad_scores, onehot, precision=lax.Precision.HIGHEST)
    grad_low = grad_scores.astype(jnp.bfloat16)
    grad_query = (
        jnp.einsum("axhtu,auxhd->atxhd", grad_low, key_heads, preferred_element_type=jnp.float32)
        * score_scale
    ).astype(jnp.bfloat16)
    grad_key = (
        jnp.einsum("axhtu,atxhd->auxhd", grad_low, query_heads, preferred_element_type=jnp.float32)
        * score_scale
    ).astype(jnp.bfloat16)
    grad_value = jnp.einsum(
        "axhtu,atxhd->auxhd", weights_low, grad_heads, preferred_element_type=jnp.float32
    ).astype(jnp.bfloat16)
    return (grad_query, grad_key, grad_value, bias_terms)


def per_device(query_vectors, key_vectors, value_vectors, grad_output, time_bias):
    head_count = time_bias.shape[0]
    frames = time_bias.shape[1]
    head_dim = query_vectors.shape[3] // head_count
    split_shape = query_vectors.shape[:3] + (head_count, head_dim)
    query_heads = query_vectors.reshape(split_shape)
    key_heads = key_vectors.reshape(split_shape)
    value_heads = value_vectors.reshape(split_shape)
    grad_heads = grad_output.reshape(split_shape)
    local_heads = head_count // lax.axis_size("tm")
    first_head = lax.axis_index("tm") * local_heads
    bias_rows = lax.dynamic_slice_in_dim(time_bias, first_head, local_heads, 0)
    grad_query, grad_key, grad_value, bias_terms = attend_back(
        lax.all_to_all(query_heads, "tm", split_axis=3, concat_axis=1, tiled=True),
        lax.all_to_all(key_heads, "tm", split_axis=3, concat_axis=1, tiled=True),
        lax.all_to_all(value_heads, "tm", split_axis=3, concat_axis=1, tiled=True),
        lax.all_to_all(grad_heads, "tm", split_axis=3, concat_axis=1, tiled=True),
        bias_rows,
    )
    grad_query, grad_key, grad_value, bias_terms = (
        lax.all_to_all(grad_query, "tm", split_axis=1, concat_axis=3, tiled=True),
        lax.all_to_all(grad_key, "tm", split_axis=1, concat_axis=3, tiled=True),
        lax.all_to_all(grad_value, "tm", split_axis=1, concat_axis=3, tiled=True),
        jnp.sum(bias_terms, axis=1),
    )
    partial_value = jnp.sum(bias_terms, axis=0)
    partial_full = lax.dynamic_update_slice_in_dim(
        jnp.zeros((head_count, frames), jnp.float32), partial_value, first_head, 0
    )
    bias_total = lax.psum(partial_full, ("tm", "patch"))
    return (
        grad_query.reshape(query_vectors.shape),
        grad_key.reshape(query_vectors.shape),
        grad_value.reshape(query_vectors.shape),
        bias_total,
    )


def solution(mesh):
    placed = (
        P(None, "tm", "patch", None),
        P(None, "tm", "patch", None),
        P(None, "tm", "patch", None),
        P(None, "tm", "patch", None),
        P(),
    )
    return jax.shard_map(
        per_device,
        mesh=mesh,
        in_specs=placed,
        out_specs=(
            P(None, "tm", "patch", None),
            P(None, "tm", "patch", None),
            P(None, "tm", "patch", None),
            P(),
        ),
        check_vma=False,
    )
```

profile of v0, /device:TPU:1, one launch (start us, length us, event | category | flops | bytes accessed | tf_op | source)
XLA Modules:
  0.0 217.6 jit_solution(1102827401183333468)
XLA Ops:
  0.6 1.2 copy.110
  2.7 10.4 %all-to-all-start.1 = ((bf16[16,1,8,16,128]{4,2,0,1,3:T(8,128)(2,1)}), bf16[16,1,8,16,128]{4,2,0,1,3:T(8,128)(2,1)S(1)}, u32[]{:S(2)}, u32[]{:S(2)}) async-start(bf16[16,1,8,16,128]{4,2,0,1,3:T(8,128)(2,1)} %copy.31), calls=%async_computation.1 | async-start | bytes 1048576 | tf_op jit(solution)/shard_map/all_to_all | solution.py:71
  14.2 8.8 %all-to-all-done.1 = bf16[16,1,8,16,128]{4,2,0,1,3:T(8,128)(2,1)S(1)} async-done(((bf16[16,1,8,16,128]{4,2,0,1,3:T(8,128)(2,1)}), bf16[16,1,8,16,128]{4,2,0,1,3:T(8,128)(2,1)S(1)}, u32[]{:S(2)}, u32[]{:S(2)}) %all-to-all-start.1) | async-done | bytes 524320 | tf_op jit(solution)/shard_map/all_to_all | solution.py:71
  23.0 4.5 %all-to-all-start.2 = ((bf16[16,1,8,16,128]{4,2,0,1,3:T(8,128)(2,1)}), bf16[16,1,8,16,128]{4,2,0,1,3:T(8,128)(2,1)S(1)}, u32[]{:S(2)}, u32[]{:S(2)}) async-start(bf16[16,1,8,16,128]{4,2,0,1,3:T(8,128)(2,1)} %copy.34), calls=%async_computation.2 | async-start | bytes 1048576 | tf_op jit(solution)/shard_map/all_to_all | solution.py:73
  28.6 8.8 %all-to-all-done.2 = bf16[16,1,8,16,128]{4,2,0,1,3:T(8,128)(2,1)S(1)} async-done(((bf16[16,1,8,16,128]{4,2,0,1,3:T(8,128)(2,1)}), bf16[16,1,8,16,128]{4,2,0,1,3:T(8,128)(2,1)S(1)}, u32[]{:S(2)}, u32[]{:S(2)}) %all-to-all-start.2) | async-done | bytes 524320 | tf_op jit(solution)/shard_map/all_to_all | solution.py:73
  37.4 4.5 %all-to-all-start = ((bf16[16,1,8,16,128]{4,2,0,1,3:T(8,128)(2,1)}), bf16[16,1,8,16,128]{4,2,0,1,3:T(8,128)(2,1)S(1)}, u32[]{:S(2)}, u32[]{:S(2)}) async-start(bf16[16,1,8,16,128]{4,2,0,1,3:T(8,128)(2,1)} %copy.29), calls=%async_computation | async-start | bytes 1048576 | tf_op jit(solution)/shard_map/all_to_all | solution.py:70
  43.1 8.7 %all-to-all-done = bf16[16,1,8,16,128]{4,2,0,1,3:T(8,128)(2,1)S(1)} async-done(((bf16[16,1,8,16,128]{4,2,0,1,3:T(8,128)(2,1)}), bf16[16,1,8,16,128]{4,2,0,1,3:T(8,128)(2,1)S(1)}, u32[]{:S(2)}, u32[]{:S(2)}) %all-to-all-start) | async-done | bytes 524320 | tf_op jit(solution)/shard_map/all_to_all | solution.py:70
  51.8 4.5 %all-to-all-start.3 = ((bf16[16,1,8,16,128]{4,2,0,1,3:T(8,128)(2,1)}), bf16[16,1,8,16,128]{4,2,0,1,3:T(8,128)(2,1)S(1)}, u32[]{:S(2)}, u32[]{:S(2)}) async-start(bf16[16,1,8,16,128]{4,2,0,1,3:T(8,128)(2,1)} %copy.36), calls=%async_computation.3 | async-start | bytes 1048576 | tf_op jit(solution)/shard_map/all_to_all | solution.py:72
  57.1 2.0 fusion.40
  59.1 7.1 %all-to-all-done.3 = bf16[16,1,8,16,128]{4,2,0,1,3:T(8,128)(2,1)S(1)} async-done(((bf16[16,1,8,16,128]{4,2,0,1,3:T(8,128)(2,1)}), bf16[16,1,8,16,128]{4,2,0,1,3:T(8,128)(2,1)S(1)}, u32[]{:S(2)}, u32[]{:S(2)}) %all-to-all-start.3) | async-done | bytes 524320 | tf_op jit(solution)/shard_map/all_to_all | solution.py:72
  66.2 2.1 fusion.8
  70.6 4.5 %all-to-all-start.4 = ((bf16[16,16,8,1,128]{4,2,0,3,1:T(8,128)(2,1)}), bf16[16,16,8,1,128]{4,2,0,3,1:T(8,128)(2,1)S(1)}, u32[]{:S(2)}, u32[]{:S(2)}) async-start(bf16[16,16,8,1,128]{4,2,0,3,1:T(8,128)(2,1)} %copy.41), calls=%async_computation.4 | async-start | bytes 1048576 | tf_op jit(solution)/shard_map/all_to_all | solution.py:77
  75.6 0.9 copy.43
  76.5 8.4 %all-to-all-done.4 = bf16[16,16,8,1,128]{4,2,0,3,1:T(8,128)(2,1)S(1)} async-done(((bf16[16,16,8,1,128]{4,2,0,3,1:T(8,128)(2,1)}), bf16[16,16,8,1,128]{4,2,0,3,1:T(8,128)(2,1)S(1)}, u32[]{:S(2)}, u32[]{:S(2)}) %all-to-all-start.4) | async-done | bytes 524320 | tf_op jit(solution)/shard_map/all_to_all | solution.py:77
  85.0 4.5 %all-to-all-start.5 = ((bf16[16,16,8,1,128]{4,2,0,3,1:T(8,128)(2,1)}), bf16[16,16,8,1,128]{4,2,0,3,1:T(8,128)(2,1)S(1)}, u32[]{:S(2)}, u32[]{:S(2)}) async-start(bf16[16,16,8,1,128]{4,2,0,3,1:T(8,128)(2,1)} %copy.43), calls=%async_computation.5 | async-start | bytes 1048576 | tf_op jit(solution)/shard_map/all_to_all | solution.py:78
  89.5 1.7 fusion.11
  91.3 0.9 copy.45
  92.2 7.2 %all-to-all-done.5 = bf16[16,16,8,1,128]{4,2,0,3,1:T(8,128)(2,1)S(1)} async-done(((bf16[16,16,8,1,128]{4,2,0,3,1:T(8,128)(2,1)}), bf16[16,16,8,1,128]{4,2,0,3,1:T(8,128)(2,1)S(1)}, u32[]{:S(2)}, u32[]{:S(2)}) %all-to-all-start.5) | async-done | bytes 524320 | tf_op jit(solution)/shard_map/all_to_all | solution.py:78
  99.4 5.1 %all-to-all-start.6 = ((bf16[16,16,8,1,128]{4,2,0,3,1:T(8,128)(2,1)}), bf16[16,16,8,1,128]{4,2,0,3,1:T(8,128)(2,1)}, u32[]{:S(2)}, u32[]{:S(2)}) async-start(bf16[16,16,8,1,128]{4,2,0,3,1:T(8,128)(2,1)} %copy.45), calls=%async_computation.6 | async-start | bytes 1048576 | tf_op jit(solution)/shard_map/all_to_all | solution.py:79
  105.7 106.8 %psum.7 = f32[16,16]{1,0:T(8,128)} all-reduce(f32[16,16]{1,0:T(8,128)S(1)} %dynamic_update_slice.3), channel_id=1, replica_groups=mesh['tm'=16,'patch'=32] {'tm','patch'}, use_global_device_ids=true, to_apply=%region_3.4 | all-reduce | flops 256 | bytes 2048 | tf_op jit(solution)/shard_map/psum | solution.py:86
  212.8 1.0 reshape.141
  214.2 1.0 reshape.142
  215.2 1.4 copy.46
  216.6 1.0 reshape.143
  (37 shorter events, 9.4 us)
Async XLA Ops:
  0.6 55.7 %copy-start = (f32[16,16]{1,0:T(8,128)S(1)}, f32[16,16]{1,0:T(8,128)}, u32[]{:S(2)}) copy-start(f32[16,16]{1,0:T(8,128)} %param.9) | copy-start | bytes 3076
  2.7 10.4 %copy-start.1 = (bf16[16,1,8,2048]{3,2,1,0:T(8,128)(2,1)S(1)}, bf16[16,1,8,2048]{3,2,1,0:T(8,128)(2,1)}, u32[]{:S(2)}) copy-start(bf16[16,1,8,2048]{3,2,1,0:T(8,128)(2,1)} %param.8) | copy-start | bytes 1572868
  2.7 20.3 %all-to-all-start.1 = ((bf16[16,1,8,16,128]{4,2,0,1,3:T(8,128)(2,1)}), bf16[16,1,8,16,128]{4,2,0,1,3:T(8,128)(2,1)S(1)}, u32[]{:S(2)}, u32[]{:S(2)}) async-start(bf16[16,1,8,16,128]{4,2,0,1,3:T(8,128)(2,1)} %copy.31), calls=%async_computation.1 | async-start | bytes 1048576 | tf_op jit(solution)/shard_map/all_to_all | solution.py:71
  14.2 13.4 %copy-start.2 = (bf16[16,1,8,2048]{3,2,1,0:T(8,128)(2,1)S(1)}, bf16[16,1,8,2048]{3,2,1,0:T(8,128)(2,1)}, u32[]{:S(2)}) copy-start(bf16[16,1,8,2048]{3,2,1,0:T(8,128)(2,1)} %param.5) | copy-start | bytes 1572868
  23.0 14.4 %all-to-all-start.2 = ((bf16[16,1,8,16,128]{4,2,0,1,3:T(8,128)(2,1)}), bf16[16,1,8,16,128]{4,2,0,1,3:T(8,128)(2,1)S(1)}, u32[]{:S(2)}, u32[]{:S(2)}) async-start(bf16[16,1,8,16,128]{4,2,0,1,3:T(8,128)(2,1)} %copy.34), calls=%async_computation.2 | async-start | bytes 1048576 | tf_op jit(solution)/shard_map/all_to_all | solution.py:73
  28.6 13.4 %copy-start.3 = (bf16[16,1,8,2048]{3,2,1,0:T(8,128)(2,1)S(1)}, bf16[16,1,8,2048]{3,2,1,0:T(8,128)(2,1)}, u32[]{:S(2)}) copy-start(bf16[16,1,8,2048]{3,2,1,0:T(8,128)(2,1)} %param.7) | copy-start | bytes 1572868
  37.4 30.9 %copy-start.4 = (bf16[16,1,8,16,128]{4,2,0,1,3:T(8,128)(2,1)}, bf16[16,1,8,16,128]{4,2,0,1,3:T(8,128)(2,1)S(1)}, u32[]{:S(2)}) copy-start(bf16[16,1,8,16,128]{4,2,0,1,3:T(8,128)(2,1)S(1)} %all-to-all-done.2) | copy-start | bytes 1572868
  37.4 14.4 %all-to-all-start = ((bf16[16,1,8,16,128]{4,2,0,1,3:T(8,128)(2,1)}), bf16[16,1,8,16,128]{4,2,0,1,3:T(8,128)(2,1)S(1)}, u32[]{:S(2)}, u32[]{:S(2)}) async-start(bf16[16,1,8,16,128]{4,2,0,1,3:T(8,128)(2,1)} %copy.29), calls=%async_computation | async-start | bytes 1048576 | tf_op jit(solution)/shard_map/all_to_all | solution.py:70
  51.8 14.4 %all-to-all-start.3 = ((bf16[16,1,8,16,128]{4,2,0,1,3:T(8,128)(2,1)}), bf16[16,1,8,16,128]{4,2,0,1,3:T(8,128)(2,1)S(1)}, u32[]{:S(2)}, u32[]{:S(2)}) async-start(bf16[16,1,8,16,128]{4,2,0,1,3:T(8,128)(2,1)} %copy.36), calls=%async_computation.3 | async-start | bytes 1048576 | tf_op jit(solution)/shard_map/all_to_all | solution.py:72
  66.2 2.1 copy-start.6
  70.6 14.4 %all-to-all-start.4 = ((bf16[16,16,8,1,128]{4,2,0,3,1:T(8,128)(2,1)}), bf16[16,16,8,1,128]{4,2,0,3,1:T(8,128)(2,1)S(1)}, u32[]{:S(2)}, u32[]{:S(2)}) async-start(bf16[16,16,8,1,128]{4,2,0,3,1:T(8,128)(2,1)} %copy.41), calls=%async_computation.4 | async-start | bytes 1048576 | tf_op jit(solution)/shard_map/all_to_all | solution.py:77
  76.5 13.0 %copy-start.5 = (bf16[16,1,8,16,128]{4,2,0,1,3:T(8,128)(2,1)S(1)}, bf16[16,1,8,16,128]{4,2,0,1,3:T(8,128)(2,1)}, u32[]{:S(2)}) copy-start(bf16[16,1,8,16,128]{4,2,0,1,3:T(8,128)(2,1)} %copy-done.4) | copy-start | bytes 1572868
  85.0 14.4 %all-to-all-start.5 = ((bf16[16,16,8,1,128]{4,2,0,3,1:T(8,128)(2,1)}), bf16[16,16,8,1,128]{4,2,0,3,1:T(8,128)(2,1)S(1)}, u32[]{:S(2)}, u32[]{:S(2)}) async-start(bf16[16,16,8,1,128]{4,2,0,3,1:T(8,128)(2,1)} %copy.43), calls=%async_computation.5 | async-start | bytes 1048576 | tf_op jit(solution)/shard_map/all_to_all | solution.py:78
  99.4 115.8 %all-to-all-start.6 = ((bf16[16,16,8,1,128]{4,2,0,3,1:T(8,128)(2,1)}), bf16[16,16,8,1,128]{4,2,0,3,1:T(8,128)(2,1)}, u32[]{:S(2)}, u32[]{:S(2)}) async-start(bf16[16,16,8,1,128]{4,2,0,3,1:T(8,128)(2,1)} %copy.45), calls=%async_computation.6 | async-start | bytes 1048576 | tf_op jit(solution)/shard_map/all_to_all | solution.py:79
where the time goes:
time: 219 us; the launch traced here: 218 us
  blocking collectives  107 us (49%)
  waiting for transfers between devices  49.1 us (22%)
  starting transfers between devices  38.1 us (17%)
  local copies, waits for them, and re-layouts  13.8 us (6%)
  matrix products  8.91 us (4%)
    psum x1, blocking collectives, per_device(): bias_total = lax.psum(partial_full, ('tm', 'patch'))  107 us
    all_to_all x1, starting transfers between devices, per_device(): lax.all_to_all(key_heads, 'tm', split_axis=3, concat_axis=1, tiled=True)  10.4 us
    all_to_all x1, waiting for transfers between devices, per_device(): lax.all_to_all(key_heads, 'tm', split_axis=3, concat_axis=1, tiled=True)  8.82 us
    all_to_all x1, waiting for transfers between devices, per_device(): lax.all_to_all(grad_heads, 'tm', split_axis=3, concat_axis=1, tiled=True)  8.82 us
    all_to_all x1, waiting for transfers between devices, per_device(): lax.all_to_all(query_heads, 'tm', split_axis=3, concat_axis=1, tiled=True)  8.74 us
    all_to_all x1, waiting for transfers between devices, per_device(): lax.all_to_all(grad_query, 'tm', split_axis=1, concat_axis=3, tiled=True)  8.44 us
    all_to_all x1, waiting for transfers between devices, per_device(): lax.all_to_all(grad_key, 'tm', split_axis=1, concat_axis=3, tiled=True)  7.19 us
    all_to_all x1, waiting for transfers between devices, per_device(): lax.all_to_all(value_heads, 'tm', split_axis=3, concat_axis=1, tiled=True)  7.13 us
  transfers between devices with their start and end apart: 7, of which 6 were waited for; matrix products, arithmetic and copies ran while one was open for 6% of the time, Pallas kernels for 0%

commit v1 on v0

v1 whole, which is shorter than its diff:
```python
import functools
import math

import jax
import jax.numpy as jnp
from jax import lax
from jax.experimental import pallas as pl
from jax.experimental.pallas import tpu as pltpu
from jax.sharding import PartitionSpec as P

MESH = pl.DeviceIdType.MESH
GROUP = 16
NEG = -1e30


def body(frames, span, parts, q_hbm, k_hbm, v_hbm, g_hbm, bias_ref, oq_hbm, ok_hbm, ov_hbm, ob_ref,
         held, back, table, acc, mine, shares, rows_all,
         in_sem, in_sent, out_sem, out_sent, share_sem, share_sent, row_sem, row_sent):
    me = lax.axis_index("tm")
    place = lax.axis_index("patch")
    rows, dim = held.shape[2], held.shape[3]
    step_rows = rows // parts
    inputs = (q_hbm, k_hbm, v_hbm, g_hbm)
    outputs = (oq_hbm, ok_hbm, ov_hbm)
    scale = 1.0 / math.sqrt(dim)

    def head_columns(head):
        return pl.ds(pl.multiple_of(head * dim, dim), dim)

    barrier = pltpu.get_barrier_semaphore()
    for off in range(1, frames):
        pl.semaphore_signal(barrier, inc=1, device_id={"tm": lax.rem(me + off, frames)}, device_id_type=MESH)
    for off in range(1, span):
        pl.semaphore_signal(barrier, inc=1, device_id={"patch": lax.rem(place + off, span)}, device_id_type=MESH)
    pl.semaphore_wait(barrier, frames - 1 + span - 1)

    def send_part(part, carry):
        part_rows = pl.ds(pl.multiple_of(part * step_rows, step_rows), step_rows)
        for a in range(4):
            pltpu.make_async_copy(
                inputs[a].at[part_rows, head_columns(me)], held.at[a, me, part_rows], in_sem.at[part]).start()
        for off in range(1, frames):
            head = lax.rem(me + off, frames)
            for a in range(4):
                pltpu.make_async_remote_copy(
                    src_ref=inputs[a].at[part_rows, head_columns(head)],
                    dst_ref=held.at[a, me, part_rows],
                    send_sem=in_sent, recv_sem=in_sem.at[part],
                    device_id={"tm": head}, device_id_type=MESH).start()
        return carry

    lax.fori_loop(0, parts, send_part, 0)

    size = frames * GROUP
    u_row = lax.broadcasted_iota(jnp.int32, (size, size), 0)
    t_col = lax.broadcasted_iota(jnp.int32, (size, size), 1)
    same = (u_row % GROUP) == (t_col % GROUP)
    offset = jnp.where(same, t_col // GROUP - u_row // GROUP, -1)
    filled = jnp.full((size, size), NEG, jnp.float32)
    for d in range(frames):
        filled = jnp.where(offset == d, bias_ref[me, d], filled)
    table[...] = filled
    acc[...] = jnp.zeros_like(acc)

    contract_last = (((1,), (1,)), ((), ()))
    contract_first = (((0,), (0,)), ((), ()))

    def attend(block):
        take = pl.ds(pl.multiple_of(block * GROUP, GROUP), GROUP)
        q, k, v, g = (held[a, :, take, :].reshape(size, dim) for a in range(4))
        scores = lax.dot_general(k, q, contract_last, preferred_element_type=jnp.float32) * scale + table[...]
        expon = jnp.exp(scores - jnp.max(scores, axis=0, keepdims=True))
        weights = expon * (1.0 / jnp.sum(expon, axis=0, keepdims=True))
        low = weights.astype(jnp.bfloat16)
        grad_weights = lax.dot_general(v, g, contract_last, preferred_element_type=jnp.float32)
        rowdot = jnp.sum(low.astype(jnp.float32) * grad_weights, axis=0, keepdims=True)
        grad_scores = weights * (grad_weights - rowdot)
        acc[...] += grad_scores
        grad_low = grad_scores.astype(jnp.bfloat16)
        dv = jnp.dot(low, g, preferred_element_type=jnp.float32)
        dk = jnp.dot(grad_low, q, preferred_element_type=jnp.float32) * scale
        dq = lax.dot_general(grad_low, k, contract_first, preferred_element_type=jnp.float32) * scale
        for a, grad in enumerate((dq, dk, dv)):
            back[a, :, take, :] = grad.astype(jnp.bfloat16).reshape(frames, GROUP, dim)

    def work_part(part, carry):
        part_rows = pl.ds(pl.multiple_of(part * step_rows, step_rows), step_rows)
        here = held.at[:, :, part_rows]
        pltpu.make_async_copy(here, here, in_sem.at[part]).wait()
        for i in range(step_rows // GROUP):
            attend(part * (step_rows // GROUP) + i)
        for off in range(1, frames):
            frame = lax.rem(me + off, frames)
            for a in range(3):
                pltpu.make_async_remote_copy(
                    src_ref=back.at[a, frame, part_rows],
                    dst_ref=outputs[a].at[part_rows, head_columns(me)],
                    send_sem=out_sent, recv_sem=out_sem.at[a],
                    device_id={"tm": frame}, device_id_type=MESH).start()
        for a in range(3):
            pltpu.make_async_copy(
                back.at[a, me, part_rows], outputs[a].at[part_rows, head_columns(me)], out_sem.at[a]).start()
        return carry

    lax.fori_loop(0, parts, work_part, 0)

    by_frame = jnp.sum(acc[...].reshape(frames, GROUP, size), axis=1)
    u_small = lax.broadcasted_iota(jnp.int32, (frames, size), 0)
    t_small = lax.broadcasted_iota(jnp.int32, (frames, size), 1) // GROUP
    lane = lax.broadcasted_iota(jnp.int32, (1, 128), 1)
    row = jnp.zeros((1, 128), jnp.float32)
    for d in range(frames):
        total = jnp.sum(jnp.where(t_small - u_small == d, by_frame, 0.0))
        row = jnp.where(lane == d, total, row)
    mine[...] = jnp.broadcast_to(row, mine.shape)
    own = pltpu.make_async_copy(mine, shares.at[place], share_sem)
    own.start()
    for off in range(1, span):
        pltpu.make_async_remote_copy(
            src_ref=mine, dst_ref=shares.at[place], send_sem=share_sent, recv_sem=share_sem,
            device_id={"patch": lax.rem(place + off, span)}, device_id_type=MESH).start()
    pltpu.make_async_copy(shares, shares, share_sem).wait()
    sent = shares.at[pl.ds(0, span - 1)]
    pltpu.make_async_copy(sent, sent, share_sent).wait()
    mine[...] = jnp.sum(shares[...], axis=0)
    own = pltpu.make_async_copy(mine, rows_all.at[me], row_sem)
    own.start()
    for off in range(1, frames):
        pltpu.make_async_remote_copy(
            src_ref=mine, dst_ref=rows_all.at[me], send_sem=row_sent, recv_sem=row_sem,
            device_id={"tm": lax.rem(me + off, frames)}, device_id_type=MESH).start()
    pltpu.make_async_copy(rows_all, rows_all, row_sem).wait()
    sent = rows_all.at[pl.ds(0, frames - 1)]
    pltpu.make_async_copy(sent, sent, row_sent).wait()
    for h in range(frames):
        ob_ref[pl.ds(h, 1), :] = rows_all[h, 0:1, 0:frames]

    sent = held.at[:, pl.ds(0, frames - 1)]
    pltpu.make_async_copy(sent, sent, in_sent).wait()
    sent = back.at[:, pl.ds(0, frames - 1)]
    pltpu.make_async_copy(sent, sent, out_sent).wait()
    for a in range(3):
        pltpu.make_async_copy(outputs[a], outputs[a], out_sem.at[a]).wait()


def per_device(span, query, key, value, grad, time_bias):
    clips, _, patches, width = query.shape
    heads, frames = time_bias.shape
    dim = width // heads
    rows = clips * patches
    flat = [item.reshape(rows, width) for item in (query, key, value, grad)]
    parts = 4
    any_space = pl.BlockSpec(memory_space=pl.ANY)
    size = frames * GROUP
    dma = pltpu.SemaphoreType.DMA
    out = pl.pallas_call(
        functools.partial(body, frames, span, parts),
        out_shape=[jax.ShapeDtypeStruct((rows, width), jnp.bfloat16)] * 3
        + [jax.ShapeDtypeStruct((heads, frames), jnp.float32)],
        in_specs=[any_space] * 4 + [pl.BlockSpec(memory_space=pltpu.SMEM)],
        out_specs=[any_space] * 3 + [pl.BlockSpec(memory_space=pltpu.VMEM)],
        scratch_shapes=[
            pltpu.VMEM((4, frames, rows, dim), jnp.bfloat16),
            pltpu.VMEM((3, frames, rows, dim), jnp.bfloat16),
            pltpu.VMEM((size, size), jnp.float32),
            pltpu.VMEM((size, size), jnp.float32),
            pltpu.VMEM((8, 128), jnp.float32),
            pltpu.VMEM((span, 8, 128), jnp.float32),
            pltpu.VMEM((frames, 8, 128), jnp.float32),
            dma((parts,)), dma, dma((3,)), dma, dma, dma, dma, dma,
        ],
        compiler_params=pltpu.CompilerParams(
            collective_id=0, has_side_effects=True, vmem_limit_bytes=40 * 2**20),
    )(*flat, time_bias)
    return tuple(item.reshape(query.shape) for item in out[:3]) + (out[3],)


def solution(mesh):
    placed = P(None, "tm", "patch", None)
    return jax.shard_map(
        functools.partial(per_device, mesh.shape["patch"]),
        mesh=mesh,
        in_specs=(placed, placed, placed, placed, P()),
        out_specs=(placed, placed, placed, P()),
        check_vma=False,
    )
```

time: 219 us -> 75.5 us (0.34)
  blocking collectives: 107 us -> 0 us
  Pallas kernels: 0 us -> 66.7 us
  waiting for transfers between devices: 49.1 us -> 0 us
  starting transfers between devices: 38.1 us -> 0 us
  matrix products: 8.91 us -> 0 us
  local copies, waits for them, and re-layouts: 13.8 us -> 7.83 us
    psum x1 -> x0, blocking collectives: 107 us -> none  [per_device(): bias_total = lax.psum(partial_full, ('tm', 'patch'))]
    pallas_call x0 -> x1, Pallas kernels: none -> 66.7 us  [per_device(): pl.pallas_call(functools.partial(body, frames, span, parts), out_shape=[j...]
    all_to_all x7 -> x0, waiting for transfers between devices: 49.1 us -> none  [the longest x1 8.82 us: per_device(): lax.all_to_all(key_heads, 'tm', split_axis=3, concat_axis=1, tiled=True)]
    all_to_all x7 -> x0, starting transfers between devices: 38.1 us -> none  [the longest x1 10.4 us: per_device(): lax.all_to_all(key_heads, 'tm', split_axis=3, concat_axis=1, tiled=True)]
    dot_general x7 -> x0, matrix products: 6.87 us -> none  [the longest x1 2.11 us: attend_back(): jnp.einsum('axhtu,auxhd->atxhd', weights_low, value_heads, preferred_elem...]
    reshape x7 -> x0, local copies, waits for them, and re-layouts: 6.79 us -> none  [the longest x1 1.02 us: per_device(): grad_key.reshape(query_vectors.shape)]
    unnamed x18 -> x14, local copies, waits for them, and re-layouts: 1.52 us -> 7.83 us
    convert_element_type x3 -> x0, local copies, waits for them, and re-layouts: 2.81 us -> none  [the longest x1 0.94 us: attend_back(): grad_value = jnp.einsum('axhtu,atxhd->auxhd', weights_low, grad_heads, pr...]
  transfers between devices with their start and end apart: 7 -> 0, of which waited for: 6 -> 0; matrix products, arithmetic and copies ran while one was open for 6% -> 0% of each run, Pallas kernels for 0% -> 0%
where the time goes in v1:
time: 75.5 us; the launch traced here: 75.2 us
  Pallas kernels  66.7 us (88%)
  local copies, waits for them, and re-layouts  7.83 us (10%)
    pallas_call x1, Pallas kernels, per_device(): pl.pallas_call(functools.partial(body, frames, span, parts), out_shape=[j...  66.7 us
    unnamed x14, local copies, waits for them, and re-layouts  7.83 us

profile of v1, /device:TPU:1, one launch (start us, length us, event | category | flops | bytes accessed | tf_op | source)
XLA Modules:
  0.0 75.2 jit_solution(12341451807582478093)
XLA Ops:
  0.6 0.0 copy-start
  0.6 1.0 %copy-done = bf16[16,1,8,2048]{3,2,1,0:T(8,128)(2,1)S(1)} copy-done((bf16[16,1,8,2048]{3,2,1,0:T(8,128)(2,1)S(1)}, bf16[16,1,8,2048]{3,2,1,0:T(8,128)(2,1)}, u32[]{:S(2)}) %copy-start) | copy-done | bytes 524312
  1.7 0.0 copy-start.1
  1.7 1.0 %copy-done.1 = bf16[16,1,8,2048]{3,2,1,0:T(8,128)(2,1)S(1)} copy-done((bf16[16,1,8,2048]{3,2,1,0:T(8,128)(2,1)S(1)}, bf16[16,1,8,2048]{3,2,1,0:T(8,128)(2,1)}, u32[]{:S(2)}) %copy-start.1) | copy-done | bytes 524312
  2.7 0.0 copy-start.2
  2.7 1.0 %copy-done.2 = bf16[16,1,8,2048]{3,2,1,0:T(8,128)(2,1)S(1)} copy-done((bf16[16,1,8,2048]{3,2,1,0:T(8,128)(2,1)S(1)}, bf16[16,1,8,2048]{3,2,1,0:T(8,128)(2,1)}, u32[]{:S(2)}) %copy-start.2) | copy-done | bytes 524312
  3.8 0.0 copy-start.3
  3.8 1.0 %copy-done.3 = bf16[16,1,8,2048]{3,2,1,0:T(8,128)(2,1)S(1)} copy-done((bf16[16,1,8,2048]{3,2,1,0:T(8,128)(2,1)S(1)}, bf16[16,1,8,2048]{3,2,1,0:T(8,128)(2,1)}, u32[]{:S(2)}) %copy-start.3) | copy-done | bytes 524312
  4.8 0.0 copy-start.4
  4.8 0.7 copy-done.4
  5.5 66.7 %shard_map.84 = (bf16[128,2048]{1,0:T(8,128)(2,1)S(1)}, bf16[128,2048]{1,0:T(8,128)(2,1)S(1)}, bf16[128,2048]{1,0:T(8,128)(2,1)S(1)}, f32[16,16]{1,0:T(8,128)S(1)}) custom-call(bf16[128,2048]{1,0:T(8,128)(2,1)S(1)} %bitcast.16, bf16[128,2048]{1,0:T(8,128)(2,1)S(1)} %bitcast.17, bf16[128,2048]{1,0:T(8,128)(2,1)S(1)} %bitcast.18, ...), custom_call_target="tpu_custom_call" | custom-call | tf_op jit(solution)/shard_map/pallas_call | solution.py:156
  72.2 0.8 %copy.16 = bf16[16,1,8,2048]{3,2,1,0:T(8,128)(2,1)} copy(bf16[16,1,8,2048]{3,2,1,0:T(8,128)(2,1)S(1)} %bitcast.15) | data formatting | bytes 1048576
  73.0 0.8 %copy.17 = bf16[16,1,8,2048]{3,2,1,0:T(8,128)(2,1)} copy(bf16[16,1,8,2048]{3,2,1,0:T(8,128)(2,1)S(1)} %bitcast.14) | data formatting | bytes 1048576
  73.8 0.8 %copy.18 = bf16[16,1,8,2048]{3,2,1,0:T(8,128)(2,1)} copy(bf16[16,1,8,2048]{3,2,1,0:T(8,128)(2,1)S(1)} %bitcast.13) | data formatting | bytes 1048576
  74.6 0.6 copy.19
Async XLA Ops:
  0.6 1.0 %copy-start = (bf16[16,1,8,2048]{3,2,1,0:T(8,128)(2,1)S(1)}, bf16[16,1,8,2048]{3,2,1,0:T(8,128)(2,1)}, u32[]{:S(2)}) copy-start(bf16[16,1,8,2048]{3,2,1,0:T(8,128)(2,1)} %param.5) | copy-start | bytes 1572868
  1.7 1.0 %copy-start.1 = (bf16[16,1,8,2048]{3,2,1,0:T(8,128)(2,1)S(1)}, bf16[16,1,8,2048]{3,2,1,0:T(8,128)(2,1)}, u32[]{:S(2)}) copy-start(bf16[16,1,8,2048]{3,2,1,0:T(8,128)(2,1)} %param.6) | copy-start | bytes 1572868
  2.7 1.0 %copy-start.2 = (bf16[16,1,8,2048]{3,2,1,0:T(8,128)(2,1)S(1)}, bf16[16,1,8,2048]{3,2,1,0:T(8,128)(2,1)}, u32[]{:S(2)}) copy-start(bf16[16,1,8,2048]{3,2,1,0:T(8,128)(2,1)} %param.7) | copy-start | bytes 1572868
  3.8 1.0 %copy-start.3 = (bf16[16,1,8,2048]{3,2,1,0:T(8,128)(2,1)S(1)}, bf16[16,1,8,2048]{3,2,1,0:T(8,128)(2,1)}, u32[]{:S(2)}) copy-start(bf16[16,1,8,2048]{3,2,1,0:T(8,128)(2,1)} %param.8) | copy-start | bytes 1572868
  4.8 0.7 copy-start.4

commit v2 on v1

v2 whole, which is shorter than its diff:
```python
import functools
import math

import jax
import jax.numpy as jnp
from jax import lax
from jax.experimental import pallas as pl
from jax.experimental.pallas import tpu as pltpu
from jax.sharding import PartitionSpec as P

MESH = pl.DeviceIdType.MESH
GROUP = 16
NEG = -1e30
FIRST, SHARER = 0, 1


def body(frames, span, parts, lag, q_hbm, k_hbm, v_hbm, g_hbm, bias_hbm, oq_hbm, ok_hbm, ov_hbm, ob_ref,
         bias_ref, held, back, table, acc, mine, gathered, group, shares, result,
         in_sem, in_sent, out_sem, out_sent, gather_sem, gather_sent, share_sem, share_sent, result_sem, result_sent,
         bias_sem, go_sem):
    me = lax.axis_index("tm")
    place = lax.axis_index("patch")
    rows, dim = held.shape[2], held.shape[3]
    step_rows = rows // parts
    inputs = (q_hbm, k_hbm, v_hbm, g_hbm)
    outputs = (oq_hbm, ok_hbm, ov_hbm)
    scale = 1.0 / math.sqrt(dim)

    def head_columns(head):
        return pl.ds(pl.multiple_of(head * dim, dim), dim)

    bias_copy = pltpu.make_async_copy(bias_hbm, bias_ref, bias_sem)
    bias_copy.start()

    barrier = pltpu.get_barrier_semaphore()
    for off in range(1, frames):
        peer = lax.rem(me + off, frames)

        @pl.when(peer != SHARER)
        def _():
            pl.semaphore_signal(barrier, inc=1, device_id={"tm": peer}, device_id_type=MESH)

    @pl.when(me == SHARER)
    def _():
        for off in range(1, span):
            pl.semaphore_signal(barrier, inc=1, device_id={"patch": lax.rem(place + off, span)}, device_id_type=MESH)

    @pl.when(me != SHARER)
    def _():
        pl.semaphore_wait(barrier, frames - 1)

    @pl.when(me == FIRST)
    def _():
        pl.semaphore_signal(go_sem, inc=1, device_id={"tm": SHARER}, device_id_type=MESH)

    @pl.when(me == SHARER)
    def _():
        pl.semaphore_wait(go_sem, 1)

    def send_part(part, carry):
        part_rows = pl.ds(pl.multiple_of(part * step_rows, step_rows), step_rows)
        for a in range(4):
            pltpu.make_async_copy(
                inputs[a].at[part_rows, head_columns(me)], held.at[a, me, part_rows], in_sem.at[part]).start()
        for off in range(1, frames):
            head = lax.rem(me + off, frames)
            for a in range(4):
                pltpu.make_async_remote_copy(
                    src_ref=inputs[a].at[part_rows, head_columns(head)],
                    dst_ref=held.at[a, me, part_rows],
                    send_sem=in_sent, recv_sem=in_sem.at[part],
                    device_id={"tm": head}, device_id_type=MESH).start()
        return carry

    lax.fori_loop(0, parts, send_part, 0)

    size = frames * GROUP
    u_row = lax.broadcasted_iota(jnp.int32, (size, size), 0)
    t_col = lax.broadcasted_iota(jnp.int32, (size, size), 1)
    same = (u_row % GROUP) == (t_col % GROUP)
    offset = jnp.where(same, t_col // GROUP - u_row // GROUP, -1)
    bias_copy.wait()
    filled = jnp.full((size, size), NEG, jnp.float32)
    for d in range(frames):
        filled = jnp.where(offset == d, bias_ref[me, d], filled)
    table[...] = filled
    acc[...] = jnp.zeros_like(acc)

    contract_last = (((1,), (1,)), ((), ()))
    contract_first = (((0,), (0,)), ((), ()))

    def attend(block):
        take = pl.ds(pl.multiple_of(block * GROUP, GROUP), GROUP)
        q, k, v, g = (held[a, :, take, :].reshape(size, dim) for a in range(4))
        scores = lax.dot_general(k, q, contract_last, preferred_element_type=jnp.float32) * scale + table[...]
        expon = jnp.exp(scores - jnp.max(scores, axis=0, keepdims=True))
        weights = expon * (1.0 / jnp.sum(expon, axis=0, keepdims=True))
        low = weights.astype(jnp.bfloat16)
        grad_weights = lax.dot_general(v, g, contract_last, preferred_element_type=jnp.float32)
        rowdot = jnp.sum(low.astype(jnp.float32) * grad_weights, axis=0, keepdims=True)
        grad_scores = weights * (grad_weights - rowdot)
        acc[...] += grad_scores
        grad_low = grad_scores.astype(jnp.bfloat16)
        dv = jnp.dot(low, g, preferred_element_type=jnp.float32)
        dk = jnp.dot(grad_low, q, preferred_element_type=jnp.float32) * scale
        dq = lax.dot_general(grad_low, k, contract_first, preferred_element_type=jnp.float32) * scale
        for a, grad in enumerate((dq, dk, dv)):
            back[a, :, take, :] = grad.astype(jnp.bfloat16).reshape(frames, GROUP, dim)

    def send_back(part, carry):
        part_rows = pl.ds(pl.multiple_of(part * step_rows, step_rows), step_rows)
        for off in range(1, frames):
            frame = lax.rem(me + off, frames)
            for a in range(3):
                pltpu.make_async_remote_copy(
                    src_ref=back.at[a, frame, part_rows],
                    dst_ref=outputs[a].at[part_rows, head_columns(me)],
                    send_sem=out_sent, recv_sem=out_sem.at[a],
                    device_id={"tm": frame}, device_id_type=MESH).start()
        for a in range(3):
            pltpu.make_async_copy(
                back.at[a, me, part_rows], outputs[a].at[part_rows, head_columns(me)], out_sem.at[a]).start()
        return carry

    def work_part(part, carry):
        here = held.at[:, :, pl.ds(pl.multiple_of(part * step_rows, step_rows), step_rows)]
        pltpu.make_async_copy(here, here, in_sem.at[part]).wait()
        for i in range(step_rows // GROUP):
            attend(part * (step_rows // GROUP) + i)

        @pl.when(part >= lag)
        def _():
            send_back(part - lag, 0)

        return carry

    lax.fori_loop(0, parts, work_part, 0)

    by_frame = jnp.sum(acc[...].reshape(frames, GROUP, size), axis=1)
    u_small = lax.broadcasted_iota(jnp.int32, (frames, size), 0)
    t_small = lax.broadcasted_iota(jnp.int32, (frames, size), 1) // GROUP
    sums = [jnp.sum(jnp.where(t_small - u_small == d, by_frame, 0.0), axis=0, keepdims=True) for d in range(frames)]
    column = jnp.sum(jnp.concatenate(sums, axis=0), axis=1, keepdims=True)
    lane = lax.broadcasted_iota(jnp.int32, mine.shape, 1)
    mine[...] = jnp.where(lane == me, column, 0.0)

    @pl.when(me != SHARER)
    def _():
        pltpu.make_async_remote_copy(
            src_ref=mine, dst_ref=gathered.at[me], send_sem=gather_sent, recv_sem=gather_sem,
            device_id={"tm": SHARER}, device_id_type=MESH).start()

    lax.fori_loop(parts - lag, parts, send_back, 0)

    @pl.when(me == SHARER)
    def _():
        pltpu.make_async_copy(mine, gathered.at[me], gather_sem).start()
        pltpu.make_async_copy(gathered, gathered, gather_sem).wait()
        group[...] = jnp.sum(gathered[...], axis=0)
        pl.semaphore_wait(barrier, span - 1)
        pltpu.make_async_copy(group, shares.at[place], share_sem).start()
        for off in range(1, span):
            pltpu.make_async_remote_copy(
                src_ref=group, dst_ref=shares.at[place], send_sem=share_sent, recv_sem=share_sem,
                device_id={"patch": lax.rem(place + off, span)}, device_id_type=MESH).start()
        pltpu.make_async_copy(shares, shares, share_sem).wait()
        result[...] = jnp.sum(shares[...], axis=0)
        for off in range(1, frames):
            pltpu.make_async_remote_copy(
                src_ref=result, dst_ref=result, send_sem=result_sent, recv_sem=result_sem,
                device_id={"tm": lax.rem(me + off, frames)}, device_id_type=MESH).start()
        sent = shares.at[pl.ds(0, span - 1)]
        pltpu.make_async_copy(sent, sent, share_sent).wait()
        sent = gathered.at[pl.ds(0, frames - 1)]
        pltpu.make_async_copy(sent, sent, result_sent).wait()

    @pl.when(me != SHARER)
    def _():
        pltpu.make_async_copy(mine, mine, gather_sent).wait()
        pltpu.make_async_copy(result, result, result_sem).wait()

    ob_ref[...] = result[...]

    sent = held.at[:, pl.ds(0, frames - 1)]
    pltpu.make_async_copy(sent, sent, in_sent).wait()
    sent = back.at[:, pl.ds(0, frames - 1)]
    pltpu.make_async_copy(sent, sent, out_sent).wait()
    for a in range(3):
        pltpu.make_async_copy(outputs[a], outputs[a], out_sem.at[a]).wait()


def finish(*refs):
    sources, targets, sem = refs[:3], refs[3:6], refs[6]
    copies = [pltpu.make_async_copy(a, b, sem.at[i]) for i, (a, b) in enumerate(zip(sources, targets))]
    for copy in copies:
        copy.start()
    for copy in copies:
        copy.wait()


def per_device(span, query, key, value, grad, time_bias):
    clips, _, patches, width = query.shape
    heads, frames = time_bias.shape
    dim = width // heads
    rows = clips * patches
    given = [item.reshape(rows, width) for item in (query, key, value, grad)] + [time_bias]
    given = [pltpu.with_memory_space_constraint(item, pltpu.HBM) for item in given]
    parts, lag = 8, 8
    any_space = pl.BlockSpec(memory_space=pl.ANY)
    size = frames * GROUP
    tile = (frames, 128)
    dma = pltpu.SemaphoreType.DMA
    out = pl.pallas_call(
        functools.partial(body, frames, span, parts, lag),
        out_shape=[jax.ShapeDtypeStruct((rows, width), jnp.bfloat16)] * 3
        + [jax.ShapeDtypeStruct(tile, jnp.float32)],
        in_specs=[any_space] * 5,
        out_specs=[any_space] * 3 + [pl.BlockSpec(memory_space=pltpu.VMEM)],
        scratch_shapes=[
            pltpu.SMEM((heads, frames), jnp.float32),
            pltpu.VMEM((4, frames, rows, dim), jnp.bfloat16),
            pltpu.VMEM((3, frames, rows, dim), jnp.bfloat16),
            pltpu.VMEM((size, size), jnp.float32),
            pltpu.VMEM((size, size), jnp.float32),
            pltpu.VMEM(tile, jnp.float32),
            pltpu.VMEM((frames,) + tile, jnp.float32),
            pltpu.VMEM(tile, jnp.float32),
            pltpu.VMEM((span,) + tile, jnp.float32),
            pltpu.VMEM(tile, jnp.float32),
            dma((parts,)), dma, dma((3,)), dma, dma, dma, dma, dma, dma, dma, dma,
            pltpu.SemaphoreType.REGULAR,
        ],
        compiler_params=pltpu.CompilerParams(
            collective_id=0, has_side_effects=True, vmem_limit_bytes=40 * 2**20),
    )(*given)
    grads = [pltpu.with_memory_space_constraint(item, pltpu.VMEM) for item in out[:3]]
    grads = pl.pallas_call(
        finish,
        out_shape=[jax.ShapeDtypeStruct((rows, width), jnp.bfloat16)] * 3,
        in_specs=[any_space] * 3,
        out_specs=[any_space] * 3,
        scratch_shapes=[dma((3,))],
        compiler_params=pltpu.CompilerParams(vmem_limit_bytes=2**20),
    )(*grads)
    return tuple(item.reshape(query.shape) for item in grads) + (out[3][:, :heads].T,)


def solution(mesh):
    placed = P(None, "tm", "patch", None)
    return jax.shard_map(
        functools.partial(per_device, mesh.shape["patch"]),
        mesh=mesh,
        in_specs=(placed, placed, placed, placed, P()),
        out_specs=(placed, placed, placed, P()),
        check_vma=False,
    )
```

time: 75.5 us -> 64.7 us (0.86)
  local copies, waits for them, and re-layouts: 7.83 us -> 0.67 us
  Pallas kernels: 66.7 us -> 63.3 us
    unnamed x14 -> x1, local copies, waits for them, and re-layouts: 7.83 us -> 0.67 us
    pallas_call x1 -> x2, Pallas kernels: 66.7 us -> 63.3 us  [the longest x1 62.1 us: per_device(): pl.pallas_call(functools.partial(body, frames, span, parts, lag), out_sha...]
where the time goes in v2:
time: 64.7 us; the launch traced here: 64.6 us
  Pallas kernels  63.3 us (98%)
  local copies, waits for them, and re-layouts  0.67 us (1%)
  between operations  0.66 us (1%)
    pallas_call x1, Pallas kernels, per_device(): pl.pallas_call(functools.partial(body, frames, span, parts, lag), out_sha...  62.1 us

profile of v2, /device:TPU:1, one launch (start us, length us, event | category | flops | bytes accessed | tf_op | source)
XLA Modules:
  0.0 64.6 jit_solution(4504012837119243505)
XLA Ops:
  0.6 62.1 %shard_map.84 = (bf16[128,2048]{1,0:T(8,128)(2,1)S(1)}, bf16[128,2048]{1,0:T(8,128)(2,1)S(1)}, bf16[128,2048]{1,0:T(8,128)(2,1)S(1)}, f32[16,128]{1,0:T(8,128)S(1)}) custom-call(bf16[128,2048]{1,0:T(8,128)(2,1)} %bitcast.15, bf16[128,2048]{1,0:T(8,128)(2,1)} %bitcast.16, bf16[128,2048]{1,0:T(8,128)(2,1)} %bitcast.17, bf16[128,2048]{1,0:T(8,128)(2,1)} %bitcast.18, ...), custom_call_target="tpu_custom_call" | custom-call | tf_op jit(solution)/shard_map/pallas_call | solution.py:213
  62.8 1.2 %shard_map.85 = (bf16[128,2048]{1,0:T(8,128)(2,1)}, bf16[128,2048]{1,0:T(8,128)(2,1)}, bf16[128,2048]{1,0:T(8,128)(2,1)}) custom-call(bf16[128,2048]{1,0:T(8,128)(2,1)S(1)} %get-tuple-element.11.refs_0_, bf16[128,2048]{1,0:T(8,128)(2,1)S(1)} %get-tuple-element.12.refs_1_, bf16[128,2048]{1,0:T(8,128)(2,1)S(1)} %get-tuple-element.13.refs_2_), custom_call_target="tpu_custom_call" | custom-call | tf_op jit(solution)/shard_map/pallas_call | solution.py:237
  63.9 0.7 %copy.12 = f32[16,16]{1,0:T(8,128)} copy(f32[16,16]{0,1:T(8,128)S(1)} %slice_bitcast_fusion) | data formatting | bytes 2048
  (1 shorter events, 0.0 us)

commit v3 on v2

v3 whole, which is shorter than its diff:
```python
import functools
import math

import jax
import jax.numpy as jnp
from jax import lax
from jax.experimental import pallas as pl
from jax.experimental.pallas import tpu as pltpu
from jax.sharding import PartitionSpec as P

MESH = pl.DeviceIdType.MESH
GROUP = 16
NEG = -1e30
FIRST, SHARER = 0, 1


def body(frames, span, parts, early, late, q_hbm, k_hbm, v_hbm, g_hbm, bias_hbm, oq_hbm, ok_hbm, ov_hbm, ob_ref,
         bias_ref, held, back, table, acc, lows, mine, shares, total, result,
         in_sem, in_sent, out_sem, out_sent, share_sem, share_sent, result_sem, result_sent,
         bias_sem, go_sem, world_sem):
    me = lax.axis_index("tm")
    place = lax.axis_index("patch")
    rows, dim = held.shape[2], held.shape[3]
    inputs = (q_hbm, k_hbm, v_hbm, g_hbm)
    outputs = (oq_hbm, ok_hbm, ov_hbm)
    scale = 1.0 / math.sqrt(dim)

    def rows_of(block):
        return pl.ds(pl.multiple_of(block * GROUP, GROUP), GROUP)

    def head_columns(head):
        return pl.ds(pl.multiple_of(head * dim, dim), dim)

    bias_copy = pltpu.make_async_copy(bias_hbm, bias_ref, bias_sem)
    bias_copy.start()

    barrier = pltpu.get_barrier_semaphore()
    for off in range(1, frames):
        peer = lax.rem(me + off, frames)

        @pl.when(peer != SHARER)
        def _():
            pl.semaphore_signal(barrier, inc=1, device_id={"tm": peer}, device_id_type=MESH)

    @pl.when(me != SHARER)
    def _():
        pl.semaphore_wait(barrier, frames - 1)

    @pl.when(me == FIRST)
    def _():
        pl.semaphore_signal(go_sem, inc=1, device_id={"tm": SHARER}, device_id_type=MESH)

    @pl.when(me == SHARER)
    def _():
        pl.semaphore_wait(go_sem, 1)
        for off in range(1, span):
            pl.semaphore_signal(barrier, inc=1, device_id={"patch": lax.rem(place + off, span)}, device_id_type=MESH)

    def send_part(part, carry):
        part_rows = rows_of(part)
        for a in range(4):
            pltpu.make_async_copy(
                inputs[a].at[part_rows, head_columns(me)], held.at[a, me, part_rows], in_sem.at[part]).start()
        for off in range(1, frames):
            head = lax.rem(me + off, frames)
            for a in range(4):
                pltpu.make_async_remote_copy(
                    src_ref=inputs[a].at[part_rows, head_columns(head)],
                    dst_ref=held.at[a, me, part_rows],
                    send_sem=in_sent, recv_sem=in_sem.at[part],
                    device_id={"tm": head}, device_id_type=MESH).start()
        return carry

    lax.fori_loop(0, parts, send_part, 0)

    size = frames * GROUP
    u_row = lax.broadcasted_iota(jnp.int32, (size, size), 0)
    t_col = lax.broadcasted_iota(jnp.int32, (size, size), 1)
    same = (u_row % GROUP) == (t_col % GROUP)
    offset = jnp.where(same, t_col // GROUP - u_row // GROUP, -1)
    bias_copy.wait()
    filled = jnp.full((size, size), NEG, jnp.float32)
    for d in range(frames):
        filled = jnp.where(offset == d, bias_ref[me, d], filled)
    table[...] = filled
    acc[...] = jnp.zeros_like(acc)

    contract_last = (((1,), (1,)), ((), ()))
    contract_first = (((0,), (0,)), ((), ()))

    def block_of(a, block):
        return held[a, :, rows_of(block), :].reshape(size, dim)

    def weigh(block):
        q, k, v, g = (block_of(a, block) for a in range(4))
        scores = lax.dot_general(k, q, contract_last, preferred_element_type=jnp.float32) * scale + table[...]
        expon = jnp.exp(scores - jnp.max(scores, axis=0, keepdims=True))
        weights = expon * (1.0 / jnp.sum(expon, axis=0, keepdims=True))
        low = weights.astype(jnp.bfloat16)
        grad_weights = lax.dot_general(v, g, contract_last, preferred_element_type=jnp.float32)
        rowdot = jnp.sum(low.astype(jnp.float32) * grad_weights, axis=0, keepdims=True)
        grad_scores = weights * (grad_weights - rowdot)
        acc[...] += grad_scores
        return low, grad_scores.astype(jnp.bfloat16)

    def gradients(block, low, grad_low):
        q, k, g = (block_of(a, block) for a in (0, 1, 3))
        dv = jnp.dot(low, g, preferred_element_type=jnp.float32)
        dk = jnp.dot(grad_low, q, preferred_element_type=jnp.float32) * scale
        dq = lax.dot_general(grad_low, k, contract_first, preferred_element_type=jnp.float32) * scale
        for a, grad in enumerate((dq, dk, dv)):
            back[a, :, rows_of(block), :] = grad.astype(jnp.bfloat16).reshape(frames, GROUP, dim)

    def send_back(part, carry):
        part_rows = rows_of(part)
        for off in range(1, frames):
            frame = lax.rem(me + off, frames)
            for a in range(3):
                pltpu.make_async_remote_copy(
                    src_ref=back.at[a, frame, part_rows],
                    dst_ref=outputs[a].at[part_rows, head_columns(me)],
                    send_sem=out_sent, recv_sem=out_sem.at[a],
                    device_id={"tm": frame}, device_id_type=MESH).start()
        for a in range(3):
            pltpu.make_async_copy(
                back.at[a, me, part_rows], outputs[a].at[part_rows, head_columns(me)], out_sem.at[a]).start()
        return carry

    def await_part(part):
        here = held.at[:, :, rows_of(part)]
        pltpu.make_async_copy(here, here, in_sem.at[part]).wait()

    def work_part(part, carry):
        await_part(part)
        gradients(part, *weigh(part))

        @pl.when(jnp.logical_and(part == parts - 2, me == SHARER))
        def _():
            pl.semaphore_wait(barrier, span - 1)
            for off in range(1, frames):
                pl.semaphore_signal(
                    world_sem, inc=1, device_id={"tm": lax.rem(me + off, frames)}, device_id_type=MESH)

        return carry

    last = parts - 1
    lax.fori_loop(0, last, work_part, 0)
    lax.fori_loop(0, early, send_back, 0)
    await_part(last)
    low, grad_low = weigh(last)
    lows[0] = low
    lows[1] = grad_low

    by_frame = jnp.sum(acc[...].reshape(frames, GROUP, size), axis=1)
    u_small = lax.broadcasted_iota(jnp.int32, (frames, size), 0)
    t_small = lax.broadcasted_iota(jnp.int32, (frames, size), 1) // GROUP
    sums = [jnp.sum(jnp.where(t_small - u_small == d, by_frame, 0.0), axis=0, keepdims=True) for d in range(frames)]
    sums += [jnp.zeros((128 - frames, size), jnp.float32)]
    mine[...] = lax.dot_general(
        jnp.ones((8, size), jnp.float32), jnp.concatenate(sums, axis=0), contract_last,
        precision=lax.Precision.HIGHEST, preferred_element_type=jnp.float32)[0:1]

    @pl.when(me != SHARER)
    def _():
        pl.semaphore_wait(world_sem, 1)

    pltpu.make_async_copy(mine, shares.at[place], share_sem).start()
    for off in sorted(range(1, span), key=lambda off: -min(off, span - off)):
        pltpu.make_async_remote_copy(
            src_ref=mine, dst_ref=shares.at[place], send_sem=share_sent, recv_sem=share_sem,
            device_id={"patch": lax.rem(place + off, span)}, device_id_type=MESH).start()
    lax.fori_loop(early, early + 1, send_back, 0)
    gradients(last, lows[0], lows[1])
    lax.fori_loop(early + 1, parts - late, send_back, 0)
    pltpu.make_async_copy(shares, shares, share_sem).wait()
    total[...] = jnp.sum(shares[...], axis=0)
    pltpu.make_async_copy(total, result.at[me], result_sem).start()
    for off in range(1, frames):
        pltpu.make_async_remote_copy(
            src_ref=total, dst_ref=result.at[me], send_sem=result_sent, recv_sem=result_sem,
            device_id={"tm": lax.rem(me + off, frames)}, device_id_type=MESH).start()
    lax.fori_loop(parts - late, parts, send_back, 0)
    pltpu.make_async_copy(result, result, result_sem).wait()
    for h in range(frames):
        ob_ref[pl.ds(h, 1), :] = result[h][:, 0:frames]
    sent = shares.at[pl.ds(0, span - 1)]
    pltpu.make_async_copy(sent, sent, share_sent).wait()
    sent = result.at[pl.ds(0, frames - 1)]
    pltpu.make_async_copy(sent, sent, result_sent).wait()

    sent = held.at[:, pl.ds(0, frames - 1)]
    pltpu.make_async_copy(sent, sent, in_sent).wait()
    sent = back.at[:, pl.ds(0, frames - 1)]
    pltpu.make_async_copy(sent, sent, out_sent).wait()
    for a in range(3):
        pltpu.make_async_copy(outputs[a], outputs[a], out_sem.at[a]).wait()


def finish(*refs):
    sources, targets, sem = refs[:4], refs[4:8], refs[8]
    copies = [pltpu.make_async_copy(a, b, sem.at[i]) for i, (a, b) in enumerate(zip(sources, targets))]
    for copy in copies:
        copy.start()
    for copy in copies:
        copy.wait()


def per_device(span, query, key, value, grad, time_bias):
    clips, _, patches, width = query.shape
    heads, frames = time_bias.shape
    dim = width // heads
    rows = clips * patches
    given = [item.reshape(rows, width) for item in (query, key, value, grad)] + [time_bias]
    given = [pltpu.with_memory_space_constraint(item, pltpu.HBM) for item in given]
    parts, early, late = rows // GROUP, 1, 1
    any_space = pl.BlockSpec(memory_space=pl.ANY)
    size = frames * GROUP
    dma = pltpu.SemaphoreType.DMA
    out = pl.pallas_call(
        functools.partial(body, frames, span, parts, early, late),
        out_shape=[jax.ShapeDtypeStruct((rows, width), jnp.bfloat16)] * 3
        + [jax.ShapeDtypeStruct((heads, frames), jnp.float32)],
        in_specs=[any_space] * 5,
        out_specs=[any_space] * 3 + [pl.BlockSpec(memory_space=pltpu.VMEM)],
        scratch_shapes=[
            pltpu.SMEM((heads, frames), jnp.float32),
            pltpu.VMEM((4, frames, rows, dim), jnp.bfloat16),
            pltpu.VMEM((3, frames, rows, dim), jnp.bfloat16),
            pltpu.VMEM((size, size), jnp.float32),
            pltpu.VMEM((size, size), jnp.float32),
            pltpu.VMEM((2, size, size), jnp.bfloat16),
            pltpu.VMEM((1, 128), jnp.float32),
            pltpu.VMEM((span, 1, 128), jnp.float32),
            pltpu.VMEM((1, 128), jnp.float32),
            pltpu.VMEM((frames, 1, 128), jnp.float32),
            dma((parts,)), dma, dma((3,)), dma, dma, dma, dma, dma, dma,
            pltpu.SemaphoreType.REGULAR, pltpu.SemaphoreType.REGULAR,
        ],
        compiler_params=pltpu.CompilerParams(
            collective_id=0, has_side_effects=True, vmem_limit_bytes=40 * 2**20),
    )(*given)
    grads = [pltpu.with_memory_space_constraint(item, pltpu.VMEM) for item in out]
    grads = pl.pallas_call(
        finish,
        out_shape=[jax.ShapeDtypeStruct(item.shape, item.dtype) for item in out],
        in_specs=[any_space] * 4,
        out_specs=[any_space] * 4,
        scratch_shapes=[dma((4,))],
        compiler_params=pltpu.CompilerParams(vmem_limit_bytes=2**20),
    )(*grads)
    return tuple(item.reshape(query.shape) for item in grads[:3]) + (grads[3],)


def solution(mesh):
    placed = P(None, "tm", "patch", None)
    return jax.shard_map(
        functools.partial(per_device, mesh.shape["patch"]),
        mesh=mesh,
        in_specs=(placed, placed, placed, placed, P()),
        out_specs=(placed, placed, placed, P()),
        check_vma=False,
    )
```

time: 64.7 us -> 56.5 us (0.87)
  Pallas kernels: 63.3 us -> 55.7 us
  local copies, waits for them, and re-layouts: 0.67 us -> 0 us
    pallas_call x2, Pallas kernels: 63.3 us -> 55.7 us  [the longest x1 54.6 us: per_device(): pl.pallas_call(functools.partial(body, frames, span, parts, early, late),...]
    unnamed x1 -> x0, local copies, waits for them, and re-layouts: 0.67 us -> none
where the time goes in v3:
time: 56.5 us; the launch traced here: 56.4 us
  Pallas kernels  55.7 us (99%)
  between operations  0.64 us (1%)
    pallas_call x1, Pallas kernels, per_device(): pl.pallas_call(functools.partial(body, frames, span, parts, early, late),...  54.6 us
    pallas_call x1, Pallas kernels, per_device(): pl.pallas_call(finish, out_shape=[jax.ShapeDtypeStruct(item.shape, item.d...  1.18 us

profile of v3, /device:TPU:1, one launch (start us, length us, event | category | flops | bytes accessed | tf_op | source)
XLA Modules:
  0.0 56.4 jit_solution(18334642938862604794)
XLA Ops:
  0.6 54.6 %shard_map.84 = (bf16[128,2048]{1,0:T(8,128)(2,1)S(1)}, bf16[128,2048]{1,0:T(8,128)(2,1)S(1)}, bf16[128,2048]{1,0:T(8,128)(2,1)S(1)}, f32[16,16]{1,0:T(8,128)S(1)}) custom-call(bf16[128,2048]{1,0:T(8,128)(2,1)} %bitcast.13, bf16[128,2048]{1,0:T(8,128)(2,1)} %bitcast.14, bf16[128,2048]{1,0:T(8,128)(2,1)} %bitcast.15, bf16[128,2048]{1,0:T(8,128)(2,1)} %bitcast.16, ...), custom_call_target="tpu_custom_call" | custom-call | tf_op jit(solution)/shard_map/pallas_call | solution.py:219
  55.2 1.2 %shard_map.85 = (bf16[128,2048]{1,0:T(8,128)(2,1)}, bf16[128,2048]{1,0:T(8,128)(2,1)}, bf16[128,2048]{1,0:T(8,128)(2,1)}, f32[16,16]{1,0:T(8,128)}) custom-call(bf16[128,2048]{1,0:T(8,128)(2,1)S(1)} %get-tuple-element.12.refs_0_, bf16[128,2048]{1,0:T(8,128)(2,1)S(1)} %get-tuple-element.13.refs_1_, bf16[128,2048]{1,0:T(8,128)(2,1)S(1)} %get-tuple-element.14.refs_2_, ...), custom_call_target="tpu_custom_call" | custom-call | tf_op jit(solution)/shard_map/pallas_call | solution.py:243

commit v4 on v3

--- a/solution.py
+++ b/solution.py
@@ -14,15 +14,14 @@
 FIRST, SHARER = 0, 1
 
 
-def body(frames, span, parts, early, late, q_hbm, k_hbm, v_hbm, g_hbm, bias_hbm, oq_hbm, ok_hbm, ov_hbm, ob_ref,
-         bias_ref, held, back, table, acc, lows, mine, shares, total, result,
-         in_sem, in_sent, out_sem, out_sent, share_sem, share_sent, result_sem, result_sent,
+def body(frames, span, parts, early, middle, q_hbm, k_hbm, v_hbm, g_hbm, bias_hbm, out, ob_ref,
+         bias_ref, stage, held, back, table, acc, lows, mine, plane, total, shares,
+         load_sem, in_sem, in_sent, out_sem, out_sent, plane_sem, plane_sent, share_sem, share_sent,
          bias_sem, go_sem, world_sem):
     me = lax.axis_index("tm")
     place = lax.axis_index("patch")
     rows, dim = held.shape[2], held.shape[3]
     inputs = (q_hbm, k_hbm, v_hbm, g_hbm)
-    outputs = (oq_hbm, ok_hbm, ov_hbm)
     scale = 1.0 / math.sqrt(dim)
 
     def rows_of(block):
@@ -33,6 +32,9 @@
 
     bias_copy = pltpu.make_async_copy(bias_hbm, bias_ref, bias_sem)
     bias_copy.start()
+    loads = [pltpu.make_async_copy(ref, stage.at[a], load_sem.at[a]) for a, ref in enumerate(inputs)]
+    for load in loads:
+        load.start()
 
     barrier = pltpu.get_barrier_semaphore()
     for off in range(1, frames):
@@ -56,19 +58,20 @@
         for off in range(1, span):
             pl.semaphore_signal(barrier, inc=1, device_id={"patch": lax.rem(place + off, span)}, device_id_type=MESH)
 
+    for load in loads:
+        load.wait()
+
     def send_part(part, carry):
         part_rows = rows_of(part)
-        for a in range(4):
-            pltpu.make_async_copy(
-                inputs[a].at[part_rows, head_columns(me)], held.at[a, me, part_rows], in_sem.at[part]).start()
+        pltpu.make_async_copy(
+            stage.at[:, part_rows, head_columns(me)], held.at[:, me, part_rows], in_sem.at[part]).start()
         for off in range(1, frames):
             head = lax.rem(me + off, frames)
-            for a in range(4):
-                pltpu.make_async_remote_copy(
-                    src_ref=inputs[a].at[part_rows, head_columns(head)],
-                    dst_ref=held.at[a, me, part_rows],
-                    send_sem=in_sent, recv_sem=in_sem.at[part],
-                    device_id={"tm": head}, device_id_type=MESH).start()
+            pltpu.make_async_remote_copy(
+                src_ref=stage.at[:, part_rows, head_columns(head)],
+                dst_ref=held.at[:, me, part_rows],
+                send_sem=in_sent, recv_sem=in_sem.at[part],
+                device_id={"tm": head}, device_id_type=MESH).start()
         return carry
 
     lax.fori_loop(0, parts, send_part, 0)
@@ -115,15 +118,12 @@
         part_rows = rows_of(part)
         for off in range(1, frames):
             frame = lax.rem(me + off, frames)
-            for a in range(3):
-                pltpu.make_async_remote_copy(
-                    src_ref=back.at[a, frame, part_rows],
-                    dst_ref=outputs[a].at[part_rows, head_columns(me)],
-                    send_sem=out_sent, recv_sem=out_sem.at[a],
-                    device_id={"tm": frame}, device_id_type=MESH).start()
-        for a in range(3):
-            pltpu.make_async_copy(
-                back.at[a, me, part_rows], outputs[a].at[part_rows, head_columns(me)], out_sem.at[a]).start()
+            pltpu.make_async_remote_copy(
+                src_ref=back.at[:, frame, part_rows],
+                dst_ref=out.at[:, part_rows, head_columns(me)],
+                send_sem=out_sent, recv_sem=out_sem,
+                device_id={"tm": frame}, device_id_type=MESH).start()
+        pltpu.make_async_copy(back.at[:, me, part_rows], out.at[:, part_rows, head_columns(me)], out_sem).start()
         return carry
 
     def await_part(part):
@@ -155,49 +155,53 @@
     u_small = lax.broadcasted_iota(jnp.int32, (frames, size), 0)
     t_small = lax.broadcasted_iota(jnp.int32, (frames, size), 1) // GROUP
     sums = [jnp.sum(jnp.where(t_small - u_small == d, by_frame, 0.0), axis=0, keepdims=True) for d in range(frames)]
-    sums += [jnp.zeros((128 - frames, size), jnp.float32)]
-    mine[...] = lax.dot_general(
-        jnp.ones((8, size), jnp.float32), jnp.concatenate(sums, axis=0), contract_last,
+    width = frames * frames
+    spread = jnp.concatenate(sums * frames, axis=0)
+    row = lax.dot_general(
+        jnp.ones((8, size), jnp.float32), spread, contract_last,
         precision=lax.Precision.HIGHEST, preferred_element_type=jnp.float32)[0:1]
+    lane = lax.broadcasted_iota(jnp.int32, (1, width), 1)
+    mine[...] = jnp.where(lane // frames == me, row, 0.0)
+
+    pltpu.make_async_copy(mine, plane.at[me], plane_sem).start()
+    for off in range(1, frames):
+        pltpu.make_async_remote_copy(
+            src_ref=mine, dst_ref=plane.at[me], send_sem=plane_sent, recv_sem=plane_sem,
+            device_id={"tm": lax.rem(me + off, frames)}, device_id_type=MESH).start()
+    gradients(last, lows[0], lows[1])
+    lax.fori_loop(early, middle, send_back, 0)
+    pltpu.make_async_copy(plane, plane, plane_sem).wait()
+    total[...] = jnp.sum(plane[...], axis=0)
 
     @pl.when(me != SHARER)
     def _():
         pl.semaphore_wait(world_sem, 1)
 
-    pltpu.make_async_copy(mine, shares.at[place], share_sem).start()
+    pltpu.make_async_copy(total, shares.at[place], share_sem).start()
     for off in sorted(range(1, span), key=lambda off: -min(off, span - off)):
         pltpu.make_async_remote_copy(
-            src_ref=mine, dst_ref=shares.at[place], send_sem=share_sent, recv_sem=share_sem,
+            src_ref=total, dst_ref=shares.at[place], send_sem=share_sent, recv_sem=share_sem,
             device_id={"patch": lax.rem(place + off, span)}, device_id_type=MESH).start()
-    lax.fori_loop(early, early + 1, send_back, 0)
-    gradients(last, lows[0], lows[1])
-    lax.fori_loop(early + 1, parts - late, send_back, 0)
+    lax.fori_loop(middle, parts, send_back, 0)
     pltpu.make_async_copy(shares, shares, share_sem).wait()
-    total[...] = jnp.sum(shares[...], axis=0)
-    pltpu.make_async_copy(total, result.at[me], result_sem).start()
-    for off in range(1, frames):
-        pltpu.make_async_remote_copy(
-            src_ref=total, dst_ref=result.at[me], send_sem=result_sent, recv_sem=result_sem,
-            device_id={"tm": lax.rem(me + off, frames)}, device_id_type=MESH).start()
-    lax.fori_loop(parts - late, parts, send_back, 0)
-    pltpu.make_async_copy(result, result, result_sem).wait()
+    table_sum = jnp.sum(shares[...], axis=0)
     for h in range(frames):
-        ob_ref[pl.ds(h, 1), :] = result[h][:, 0:frames]
+        ob_ref[pl.ds(h, 1), :] = table_sum[:, h * frames : (h + 1) * frames]
+    sent = plane.at[pl.ds(0, frames - 1)]
+    pltpu.make_async_copy(sent, sent, plane_sent).wait()
     sent = shares.at[pl.ds(0, span - 1)]
     pltpu.make_async_copy(sent, sent, share_sent).wait()
-    sent = result.at[pl.ds(0, frames - 1)]
-    pltpu.make_async_copy(sent, sent, result_sent).wait()
 
     sent = held.at[:, pl.ds(0, frames - 1)]
     pltpu.make_async_copy(sent, sent, in_sent).wait()
     sent = back.at[:, pl.ds(0, frames - 1)]
     pltpu.make_async_copy(sent, sent, out_sent).wait()
-    for a in range(3):
-        pltpu.make_async_copy(outputs[a], outputs[a], out_sem.at[a]).wait()
+    pltpu.make_async_copy(out, out, out_sem).wait()
 
 
 def finish(*refs):
-    sources, targets, sem = refs[:4], refs[4:8], refs[8]
+    grads, bias, targets, sem = refs[0], refs[1], refs[2:6], refs[6]
+    sources = [grads.at[a] for a in range(3)] + [bias]
     copies = [pltpu.make_async_copy(a, b, sem.at[i]) for i, (a, b) in enumerate(zip(sources, targets))]
     for copy in copies:
         copy.start()
@@ -212,28 +216,29 @@
     rows = clips * patches
     given = [item.reshape(rows, width) for item in (query, key, value, grad)] + [time_bias]
     given = [pltpu.with_memory_space_constraint(item, pltpu.HBM) for item in given]
-    parts, early, late = rows // GROUP, 1, 1
+    parts, early, middle = rows // GROUP, 1, 3
     any_space = pl.BlockSpec(memory_space=pl.ANY)
     size = frames * GROUP
     dma = pltpu.SemaphoreType.DMA
     out = pl.pallas_call(
-        functools.partial(body, frames, span, parts, early, late),
-        out_shape=[jax.ShapeDtypeStruct((rows, width), jnp.bfloat16)] * 3
-        + [jax.ShapeDtypeStruct((heads, frames), jnp.float32)],
+        functools.partial(body, frames, span, parts, early, middle),
+        out_shape=[
+            jax.ShapeDtypeStruct((3, rows, width), jnp.bfloat16), jax.ShapeDtypeStruct((heads, frames), jnp.float32)],
         in_specs=[any_space] * 5,
-        out_specs=[any_space] * 3 + [pl.BlockSpec(memory_space=pltpu.VMEM)],
+        out_specs=[any_space] + [pl.BlockSpec(memory_space=pltpu.VMEM)],
         scratch_shapes=[
             pltpu.SMEM((heads, frames), jnp.float32),
+            pltpu.VMEM((4, rows, width), jnp.bfloat16),
             pltpu.VMEM((4, frames, rows, dim), jnp.bfloat16),
             pltpu.VMEM((3, frames, rows, dim), jnp.bfloat16),
             pltpu.VMEM((size, size), jnp.float32),
             pltpu.VMEM((size, size), jnp.float32),
             pltpu.VMEM((2, size, size), jnp.bfloat16),
-            pltpu.VMEM((1, 128), jnp.float32),
-            pltpu.VMEM((span, 1, 128), jnp.float32),
-            pltpu.VMEM((1, 128), jnp.float32),
-            pltpu.VMEM((frames, 1, 128), jnp.float32),
-            dma((parts,)), dma, dma((3,)), dma, dma, dma, dma, dma, dma,
+            pltpu.VMEM((1, heads * frames), jnp.float32),
+            pltpu.VMEM((frames, 1, heads * frames), jnp.float32),
+            pltpu.VMEM((1, heads * frames), jnp.float32),
+            pltpu.VMEM((span, 1, heads * frames), jnp.float32),
+            dma((4,)), dma((parts,)), dma, dma, dma, dma, dma, dma, dma, dma,
             pltpu.SemaphoreType.REGULAR, pltpu.SemaphoreType.REGULAR,
         ],
         compiler_params=pltpu.CompilerParams(
@@ -242,8 +247,9 @@
     grads = [pltpu.with_memory_space_constraint(item, pltpu.VMEM) for item in out]
     grads = pl.pallas_call(
         finish,
-        out_shape=[jax.ShapeDtypeStruct(item.shape, item.dtype) for item in out],
-        in_specs=[any_space] * 4,
+        out_shape=[jax.ShapeDtypeStruct((rows, width), jnp.bfloat16)] * 3
+        + [jax.ShapeDtypeStruct((heads, frames), jnp.float32)],
+        in_specs=[any_space] * 2,
         out_specs=[any_space] * 4,
         scratch_shapes=[dma((4,))],
         compiler_params=pltpu.CompilerParams(vmem_limit_bytes=2**20),

time: 56.5 us -> 55.8 us (0.988)
  Pallas kernels: 55.7 us -> 55 us
    pallas_call x2, Pallas kernels: 55.7 us -> 55 us  [the longest x1 53.8 us: per_device(): pl.pallas_call(functools.partial(body, frames, span, parts, early, middle...]
where the time goes in v4:
time: 55.8 us; the launch traced here: 55.6 us
  Pallas kernels  55 us (99%)
  between operations  0.64 us (1%)
    pallas_call x1, Pallas kernels, per_device(): pl.pallas_call(functools.partial(body, frames, span, parts, early, middle...  53.8 us
    pallas_call x1, Pallas kernels, per_device(): pl.pallas_call(finish, out_shape=[jax.ShapeDtypeStruct((rows, width), jnp...  1.18 us

profile of v4, /device:TPU:1, one launch (start us, length us, event | category | flops | bytes accessed | tf_op | source)
XLA Modules:
  0.0 55.6 jit_solution(12777659341671326269)
XLA Ops:
  0.6 53.8 %shard_map.84 = (bf16[3,128,2048]{2,1,0:T(8,128)(2,1)S(1)}, f32[16,16]{1,0:T(8,128)S(1)}) custom-call(bf16[128,2048]{1,0:T(8,128)(2,1)} %bitcast.13, bf16[128,2048]{1,0:T(8,128)(2,1)} %bitcast.14, bf16[128,2048]{1,0:T(8,128)(2,1)} %bitcast.15, bf16[128,2048]{1,0:T(8,128)(2,1)} %bitcast.16, f32[16,16]{1,0:T(8,128)} %bias_hbm.1), custom_call_target="tpu_custom_call" | custom-call | tf_op jit(solution)/shard_map/pallas_call | solution.py:223
  54.4 1.2 %shard_map.85 = (bf16[128,2048]{1,0:T(8,128)(2,1)}, bf16[128,2048]{1,0:T(8,128)(2,1)}, bf16[128,2048]{1,0:T(8,128)(2,1)}, f32[16,16]{1,0:T(8,128)}) custom-call(bf16[3,128,2048]{2,1,0:T(8,128)(2,1)S(1)} %get-tuple-element.10.refs_0_, f32[16,16]{1,0:T(8,128)S(1)} %get-tuple-element.11.refs_1_), custom_call_target="tpu_custom_call" | custom-call | tf_op jit(solution)/shard_map/pallas_call | solution.py:248

commit v5 on v4

--- a/solution.py
+++ b/solution.py
@@ -163,33 +163,34 @@
     lane = lax.broadcasted_iota(jnp.int32, (1, width), 1)
     mine[...] = jnp.where(lane // frames == me, row, 0.0)
 
-    pltpu.make_async_copy(mine, plane.at[me], plane_sem).start()
-    for off in range(1, frames):
+    @pl.when(me != SHARER)
+    def _():
+        pl.semaphore_wait(world_sem, 1)
+
+    side, z = lax.rem(place, 2), place // 2
+    pltpu.make_async_copy(mine, plane.at[side * frames + me], plane_sem).start()
+    for other, off in [(1, off) for off in range(frames)] + [(0, off) for off in range(1, frames)]:
+        target = {"tm": lax.rem(me + off, frames), "patch": 2 * z + lax.rem(side + other, 2)}
         pltpu.make_async_remote_copy(
-            src_ref=mine, dst_ref=plane.at[me], send_sem=plane_sent, recv_sem=plane_sem,
-            device_id={"tm": lax.rem(me + off, frames)}, device_id_type=MESH).start()
+            src_ref=mine, dst_ref=plane.at[side * frames + me], send_sem=plane_sent, recv_sem=plane_sem,
+            device_id=target, device_id_type=MESH).start()
     gradients(last, lows[0], lows[1])
     lax.fori_loop(early, middle, send_back, 0)
     pltpu.make_async_copy(plane, plane, plane_sem).wait()
     total[...] = jnp.sum(plane[...], axis=0)
-
-    @pl.when(me != SHARER)
-    def _():
-        pl.semaphore_wait(world_sem, 1)
-
-    pltpu.make_async_copy(total, shares.at[place], share_sem).start()
-    for off in sorted(range(1, span), key=lambda off: -min(off, span - off)):
+    pltpu.make_async_copy(total, shares.at[z], share_sem).start()
+    for off in sorted(range(1, span // 2), key=lambda off: -min(off, span // 2 - off)):
         pltpu.make_async_remote_copy(
-            src_ref=total, dst_ref=shares.at[place], send_sem=share_sent, recv_sem=share_sem,
-            device_id={"patch": lax.rem(place + off, span)}, device_id_type=MESH).start()
+            src_ref=total, dst_ref=shares.at[z], send_sem=share_sent, recv_sem=share_sem,
+            device_id={"patch": 2 * lax.rem(z + off, span // 2) + side}, device_id_type=MESH).start()
     lax.fori_loop(middle, parts, send_back, 0)
     pltpu.make_async_copy(shares, shares, share_sem).wait()
     table_sum = jnp.sum(shares[...], axis=0)
     for h in range(frames):
         ob_ref[pl.ds(h, 1), :] = table_sum[:, h * frames : (h + 1) * frames]
-    sent = plane.at[pl.ds(0, frames - 1)]
+    sent = plane.at[pl.ds(0, 2 * frames - 1)]
     pltpu.make_async_copy(sent, sent, plane_sent).wait()
-    sent = shares.at[pl.ds(0, span - 1)]
+    sent = shares.at[pl.ds(0, span // 2 - 1)]
     pltpu.make_async_copy(sent, sent, share_sent).wait()
 
     sent = held.at[:, pl.ds(0, frames - 1)]
@@ -235,9 +236,9 @@
             pltpu.VMEM((size, size), jnp.float32),
             pltpu.VMEM((2, size, size), jnp.bfloat16),
             pltpu.VMEM((1, heads * frames), jnp.float32),
-            pltpu.VMEM((frames, 1, heads * frames), jnp.float32),
+            pltpu.VMEM((2 * frames, 1, heads * frames), jnp.float32),
             pltpu.VMEM((1, heads * frames), jnp.float32),
-            pltpu.VMEM((span, 1, heads * frames), jnp.float32),
+            pltpu.VMEM((span // 2, 1, heads * frames), jnp.float32),
             dma((4,)), dma((parts,)), dma, dma, dma, dma, dma, dma, dma, dma,
             pltpu.SemaphoreType.REGULAR, pltpu.SemaphoreType.REGULAR,
         ],

time: 55.8 us -> 55.5 us (level)
  no operation moved by 1% of the time
where the time goes in v5:
time: 55.5 us; the launch traced here: 55.4 us
  Pallas kernels  54.7 us (99%)
  between operations  0.64 us (1%)
    pallas_call x1, Pallas kernels, per_device(): pl.pallas_call(functools.partial(body, frames, span, parts, early, middle...  53.6 us
    pallas_call x1, Pallas kernels, per_device(): pl.pallas_call(finish, out_shape=[jax.ShapeDtypeStruct((rows, width), jnp...  1.18 us

profile of v5, /device:TPU:1, one launch (start us, length us, event | category | flops | bytes accessed | tf_op | source)
XLA Modules:
  0.0 55.4 jit_solution(6772282585344542628)
XLA Ops:
  0.6 53.6 %shard_map.84 = (bf16[3,128,2048]{2,1,0:T(8,128)(2,1)S(1)}, f32[16,16]{1,0:T(8,128)S(1)}) custom-call(bf16[128,2048]{1,0:T(8,128)(2,1)} %bitcast.13, bf16[128,2048]{1,0:T(8,128)(2,1)} %bitcast.14, bf16[128,2048]{1,0:T(8,128)(2,1)} %bitcast.15, bf16[128,2048]{1,0:T(8,128)(2,1)} %bitcast.16, f32[16,16]{1,0:T(8,128)} %bias_hbm.1), custom_call_target="tpu_custom_call" | custom-call | tf_op jit(solution)/shard_map/pallas_call | solution.py:224
  54.2 1.2 %shard_map.85 = (bf16[128,2048]{1,0:T(8,128)(2,1)}, bf16[128,2048]{1,0:T(8,128)(2,1)}, bf16[128,2048]{1,0:T(8,128)(2,1)}, f32[16,16]{1,0:T(8,128)}) custom-call(bf16[3,128,2048]{2,1,0:T(8,128)(2,1)S(1)} %get-tuple-element.10.refs_0_, f32[16,16]{1,0:T(8,128)S(1)} %get-tuple-element.11.refs_1_), custom_call_target="tpu_custom_call" | custom-call | tf_op jit(solution)/shard_map/pallas_call | solution.py:249

commit v6 on v5

--- a/solution.py
+++ b/solution.py
@@ -32,9 +32,10 @@
 
     bias_copy = pltpu.make_async_copy(bias_hbm, bias_ref, bias_sem)
     bias_copy.start()
-    loads = [pltpu.make_async_copy(ref, stage.at[a], load_sem.at[a]) for a, ref in enumerate(inputs)]
-    for load in loads:
-        load.start()
+    first_rows, other_rows = pl.ds(0, GROUP), pl.ds(GROUP, rows - GROUP)
+    for i, some in enumerate((first_rows, other_rows)):
+        for a, ref in enumerate(inputs):
+            pltpu.make_async_copy(ref.at[some], stage.at[a, some], load_sem.at[i]).start()
 
     barrier = pltpu.get_barrier_semaphore()
     for off in range(1, frames):
@@ -57,9 +58,6 @@
         pl.semaphore_wait(go_sem, 1)
         for off in range(1, span):
             pl.semaphore_signal(barrier, inc=1, device_id={"patch": lax.rem(place + off, span)}, device_id_type=MESH)
-
-    for load in loads:
-        load.wait()
 
     def send_part(part, carry):
         part_rows = rows_of(part)
@@ -74,7 +72,12 @@
                 device_id={"tm": head}, device_id_type=MESH).start()
         return carry
 
-    lax.fori_loop(0, parts, send_part, 0)
+    here = stage.at[:, first_rows]
+    pltpu.make_async_copy(here, here, load_sem.at[0]).wait()
+    send_part(0, 0)
+    here = stage.at[:, other_rows]
+    pltpu.make_async_copy(here, here, load_sem.at[1]).wait()
+    lax.fori_loop(1, parts, send_part, 0)
 
     size = frames * GROUP
     u_row = lax.broadcasted_iota(jnp.int32, (size, size), 0)
@@ -239,7 +242,7 @@
             pltpu.VMEM((2 * frames, 1, heads * frames), jnp.float32),
             pltpu.VMEM((1, heads * frames), jnp.float32),
             pltpu.VMEM((span // 2, 1, heads * frames), jnp.float32),
-            dma((4,)), dma((parts,)), dma, dma, dma, dma, dma, dma, dma, dma,
+            dma((2,)), dma((parts,)), dma, dma, dma, dma, dma, dma, dma, dma,
             pltpu.SemaphoreType.REGULAR, pltpu.SemaphoreType.REGULAR,
         ],
         compiler_params=pltpu.CompilerParams(

time: 55.5 us -> 55.5 us (level)
  no operation moved by 1% of the time
where the time goes in v6:
time: 55.5 us; the launch traced here: 55.3 us
  Pallas kernels  54.7 us (99%)
  between operations  0.64 us (1%)
    pallas_call x1, Pallas kernels, per_device(): pl.pallas_call(functools.partial(body, frames, span, parts, early, middle...  53.5 us
    pallas_call x1, Pallas kernels, per_device(): pl.pallas_call(finish, out_shape=[jax.ShapeDtypeStruct((rows, width), jnp...  1.18 us

profile of v6, /device:TPU:1, one launch (start us, length us, event | category | flops | bytes accessed | tf_op | source)
XLA Modules:
  0.0 55.3 jit_solution(14921021648245633759)
XLA Ops:
  0.6 53.5 %shard_map.84 = (bf16[3,128,2048]{2,1,0:T(8,128)(2,1)S(1)}, f32[16,16]{1,0:T(8,128)S(1)}) custom-call(bf16[128,2048]{1,0:T(8,128)(2,1)} %bitcast.13, bf16[128,2048]{1,0:T(8,128)(2,1)} %bitcast.14, bf16[128,2048]{1,0:T(8,128)(2,1)} %bitcast.15, bf16[128,2048]{1,0:T(8,128)(2,1)} %bitcast.16, f32[16,16]{1,0:T(8,128)} %bias_hbm.1), custom_call_target="tpu_custom_call" | custom-call | tf_op jit(solution)/shard_map/pallas_call | solution.py:227
  54.1 1.2 %shard_map.85 = (bf16[128,2048]{1,0:T(8,128)(2,1)}, bf16[128,2048]{1,0:T(8,128)(2,1)}, bf16[128,2048]{1,0:T(8,128)(2,1)}, f32[16,16]{1,0:T(8,128)}) custom-call(bf16[3,128,2048]{2,1,0:T(8,128)(2,1)S(1)} %get-tuple-element.10.refs_0_, f32[16,16]{1,0:T(8,128)S(1)} %get-tuple-element.11.refs_1_), custom_call_target="tpu_custom_call" | custom-call | tf_op jit(solution)/shard_map/pallas_call | solution.py:252
